TPU v7x, 32 devices: a whole 2x2x4 slice. The times are simulated.
32 devices in a mesh: seq: 4 (over z), wide: 8 (over y, x, core).
Axes of the slice: x: 2, y: 2, z: 4, core: 2. Of those that a mesh axis runs over, the one named last changes fastest.
Arguments:
- layer_input: bfloat16 [8192, 8192], P(('wide', 'seq')), may hold values from -6 to 6
- head_inputs: bfloat16 [8192, 8192], P(('wide', 'seq')), may hold values from -6 to 6
- output_grad: bfloat16 [8192, 8192], P(('wide', 'seq')), may hold values from -6 to 6
- step_raw: bfloat16 [8192, 128], P(('wide', 'seq'))
- state_write: bfloat16 [8192, 64], P(('wide', 'seq')), may hold values from -5 to 5
- state_read: bfloat16 [8192, 64], P(('wide', 'seq')), may hold values from -5 to 5
- decay_log: float32 [128], replicated
- step_bias: float32 [128], replicated, may hold values from -1 to 0.5
- skip_gain: float32 [128], replicated, may hold values from 0.5 to 1.5
Outputs:
- grad_x: bfloat16 [8192, 8192], P(('wide', 'seq'))
- weight_grad: float32 [8192, 256], P(('seq', 'wide'))
All inputs are finite; a program needn't handle non-finite values.
Results may differ from a plain program's by a relative error of at most 0.0029.
Values may be sent and summed in bfloat16 or wider, within the bound.
No kernel may reach another device: no remote copies, remote signals or barrier semaphores. Data moves between devices by JAX's collectives and lax.ppermute only.
A program may use at most 384 MiB of HBM per device.

v0:
```python
import functools
import math

import jax
import jax.numpy as jnp
from jax import lax
from jax.experimental import pallas as pl
from jax.experimental.pallas import tpu as pltpu
from jax.sharding import PartitionSpec as P

F32 = jnp.float32
BF16 = jnp.bfloat16
EXACT = lax.Precision.HIGHEST
VMEM_LIMIT = 56 * 1024 * 1024
TOP_POWER = 30.0
PRODUCT_BOUND = 30.0
CARRY_HEADS = 16
PAIR_HEADS = 8
META = 16
HALVES = 2


def mul(a, b):
    return lax.dot_general(a, b, (((1,), (0,)), ((), ())), preferred_element_type=F32)


def mul_nt(a, b):
    return lax.dot_general(a, b, (((1,), (1,)), ((), ())), preferred_element_type=F32)


def mul_exact(a, b, dims=((1,), (0,))):
    return lax.dot_general(a, b, (dims, ((), ())), preferred_element_type=F32, precision=EXACT)


def halves(value):
    top = value.astype(BF16)
    return top, (value - top.astype(F32)).astype(BF16)


def power_for(bound):
    power = jnp.floor(TOP_POWER - jnp.log2(jnp.maximum(bound, 1e-37)))
    return jnp.clip(power, -100.0, 100.0)


def thirds(value):
    top, rest = value.astype(BF16), value
    rest = rest - top.astype(F32)
    middle = rest.astype(BF16)
    return top, middle, (rest - middle.astype(F32)).astype(BF16)


def encode(value):
    square = value * value
    fourth = square * square
    return jnp.where(value < 0, -fourth, fourth).astype(BF16)


def decode(coded):
    coded = coded.astype(F32)
    size = jnp.maximum(jnp.abs(coded), 1e-37)
    inverse = lax.rsqrt(size)
    return coded * inverse * lax.rsqrt(size * inverse)


def head_selector(first_head, heads, lanes, head_width):
    row = lax.broadcasted_iota(jnp.int32, (heads, lanes), 0)
    lane = lax.broadcasted_iota(jnp.int32, (heads, lanes), 1)
    return jnp.where(row == first_head + lane // head_width, 1.0, 0.0).astype(BF16)


def triangle(length, keep):
    row = lax.broadcasted_iota(jnp.int32, (length, length), 0)
    col = lax.broadcasted_iota(jnp.int32, (length, length), 1)
    return jnp.where(keep(row, col), 1.0, 0.0).astype(F32)


def summary_kernel(
    head_width,
    first_head,
    raw_ref,
    bias_ref,
    decay_ref,
    write_ref,
    read_ref,
    x_ref,
    dy_ref,
    message_ref,
    step_ref,
    cum_ref,
    weight_f,
    weight_b,
    facts,
):
    turn = pl.program_id(0)
    heads = raw_ref.shape[1]
    rows, lanes = x_ref.shape
    state = write_ref.shape[0]

    @pl.when(turn == 0)
    def _():
        step = jax.nn.softplus(raw_ref[...].astype(F32) + bias_ref[...])
        rate = -jnp.exp(decay_ref[...])
        cum = mul_exact(triangle(rows, lambda r, c: r >= c), step * rate)
        finish = cum[rows - 1 : rows, :]
        forward = step * jnp.exp(finish - cum)
        backward = jnp.exp(cum)
        power_f = power_for(PRODUCT_BOUND * jnp.sum(forward, axis=0, keepdims=True))
        power_b = power_for(PRODUCT_BOUND * jnp.sum(backward, axis=0, keepdims=True))
        step_ref[...] = step
        cum_ref[...] = cum
        parts = thirds(jnp.maximum(finish, -1e30))
        facts[...] = jnp.concatenate(
            [part.astype(F32) for part in parts]
            + [power_f, power_b, jnp.zeros((META - 5, heads), F32)],
            axis=0,
        ).astype(BF16)
        top, low = halves(forward * jnp.exp2(power_f))
        weight_f[...] = jnp.concatenate([top, low], axis=1)
        top, low = halves(backward * jnp.exp2(power_b))
        weight_b[...] = jnp.concatenate([top, low], axis=1)

    pick = head_selector(first_head + turn * (lanes // head_width), heads, lanes, head_width)
    pick_twice = jnp.concatenate([pick, pick], axis=0)
    width = message_ref.shape[2]

    def put(start, value):
        for owner in range(message_ref.shape[0]):
            message_ref[owner, start : start + value.shape[0], :] = value[
                :, owner * width : (owner + 1) * width
            ]

    def summed(tokens_ref, weight, rows_t):
        top, low = halves(tokens_ref[...].astype(F32) * mul(weight[...], pick_twice))
        return encode(mul(rows_t[...], top) + mul(rows_t[...], low))

    put(0, summed(x_ref, weight_f, write_ref))
    put(state, summed(dy_ref, weight_b, read_ref))
    put(2 * state, mul(facts[...], pick).astype(BF16))


def scan_kernel(message_ref, answer_ref, powers):
    blocks, double, lanes = message_ref.shape
    state = (double - META) // 2
    top = 2.0**TOP_POWER

    def one(block, start, power_row, side, running, bound):
        facts = message_ref[block, 2 * state : double, :].astype(F32)
        decay = jnp.exp(facts[0:1] + facts[1:2] + facts[2:3])
        back = jnp.exp2(-facts[power_row : power_row + 1])
        power = power_for(bound)
        powers[side, pl.ds(block, 1), :] = power
        answer_ref[block, start : start + state, :] = encode(running * jnp.exp2(power))
        own = decode(message_ref[block, start : start + state, :]) * back
        return running * decay + own, bound * decay + top * back

    def both(block, carry):
        ahead, ahead_bound, behind, behind_bound = carry
        return one(block, 0, 3, 0, ahead, ahead_bound) + one(
            blocks - 1 - block, state, 4, 1, behind, behind_bound
        )

    zero, none = jnp.zeros((state, lanes), F32), jnp.zeros((1, lanes), F32)
    lax.fori_loop(0, blocks, both, (zero, none, zero, none), unroll=4)
    row = lax.broadcasted_iota(jnp.int32, (blocks, META, lanes), 1)
    ahead, behind = powers[0][:, None, :], powers[1][:, None, :]
    meta = jnp.where(row == 0, ahead, jnp.where(row == 1, behind, 0.0))
    answer_ref[:, 2 * state : double, :] = meta.astype(BF16)


def block_kernel(
    head_width,
    scale,
    first_head,
    step_ref,
    cum_ref,
    write_ref,
    read_ref,
    x_ref,
    dy_ref,
    inner_ref,
    own_ref,
    within_ref,
    maps_ref,
    read_write,
    source,
    cum_rows,
    pair_sum,
    out_flow,
):
    turn = pl.program_id(0)
    rows, lanes = x_ref.shape
    half = rows // 2
    heads = step_ref.shape[1]
    group = lanes // head_width

    @pl.when(turn == 0)
    def _():
        read_write[...] = scale * lax.dot_general(
            write_ref[...], read_ref[...], (((0,), (0,)), ((), ())), preferred_element_type=F32
        )
        source[...] = jnp.log(step_ref[...]) - cum_ref[...]
        cum_rows[...] = cum_ref[...].T
        pair_sum[...] = jnp.zeros_like(pair_sum)
        out_flow[...] = jnp.zeros_like(out_flow)
        own_ref[...] = jnp.zeros_like(own_ref)

    first = first_head + turn * group
    near = pltpu.roll(source[...], lax.rem(heads - first, heads), axis=1)
    near_cum = cum_rows[pl.ds(first, group), :]
    row = lax.broadcasted_iota(jnp.int32, (half, half), 0)
    col = lax.broadcasted_iota(jnp.int32, (half, half), 1)
    ahead = col >= row
    lane = lax.broadcasted_iota(jnp.int32, (half, 2 * head_width), 1)
    first_half = lane < head_width
    head_lane = lax.broadcasted_iota(jnp.int32, (half, heads), 1)
    flow_aa = read_write[0:half, 0:half]
    flow_ab = read_write[0:half, half:rows]
    flow_bb = read_write[half:rows, half:rows]
    sum_aa = jnp.zeros((half, half), F32)
    sum_ab = jnp.zeros((half, half), F32)
    sum_bb = jnp.zeros((half, half), F32)
    own_a = jnp.zeros((half, heads), F32)
    own_b = jnp.zeros((half, heads), F32)
    zero = jnp.zeros((half, 2 * head_width), BF16)
    flows = []
    for pair in range(group // 2):
        span = slice(pair * 2 * head_width, (pair + 1) * 2 * head_width)
        x_a, x_b = x_ref[0:half, span], x_ref[half:rows, span]
        dy_a, dy_b = dy_ref[0:half, span], dy_ref[half:rows, span]
        early_a, late_a = jnp.where(first_half, dy_a, zero), jnp.where(first_half, zero, dy_a)
        early_b, late_b = jnp.where(first_half, dy_b, zero), jnp.where(first_half, zero, dy_b)
        stack = jnp.concatenate([early_a, early_b, late_a, late_b], axis=0)
        stack_b = jnp.concatenate([early_b, late_b], axis=0)
        grad_a = mul_nt(x_a, stack)
        grad_b = mul_nt(x_b, stack_b)
        masks_a, masks_b = [], []
        for side in range(2):
            place = pair * 2 + side
            head = first + place
            from_a = near[0:half, place : place + 1]
            from_b = near[half:rows, place : place + 1]
            to_a = near_cum[place : place + 1, 0:half]
            to_b = near_cum[place : place + 1, half:rows]
            fade_aa = jnp.exp(jnp.where(ahead, to_a + from_a, -1e30))
            fade_ab = jnp.exp(to_b + from_a)
            fade_bb = jnp.exp(jnp.where(ahead, to_b + from_b, -1e30))
            weigh_aa = fade_aa * grad_a[:, side * rows : side * rows + half]
            weigh_ab = fade_ab * grad_a[:, side * rows + half : (side + 1) * rows]
            weigh_bb = fade_bb * grad_b[:, side * half : (side + 1) * half]
            sum_aa += weigh_aa
            sum_ab += weigh_ab
            sum_bb += weigh_bb
            masks_a += [(fade_aa * flow_aa).astype(BF16), (fade_ab * flow_ab).astype(BF16)]
            masks_b += [(fade_bb * flow_bb).astype(BF16)]
            pair_aa = weigh_aa * flow_aa
            pair_ab = weigh_ab * flow_ab
            pair_bb = weigh_bb * flow_bb
            flow_out = jnp.sum(pair_aa + pair_ab, axis=1, keepdims=True)
            own_a = jnp.where(head_lane == head, flow_out, own_a)
            flow_out = jnp.sum(pair_bb, axis=1, keepdims=True)
            own_b = jnp.where(head_lane == head, flow_out, own_b)
            flow_in = [
                jnp.sum(pair_aa, axis=0, keepdims=True),
                jnp.sum(pair_ab, axis=0, keepdims=True) + jnp.sum(pair_bb, axis=0, keepdims=True),
            ]
            flows.append(jnp.concatenate(flow_in, axis=1))
        inner_ref[0:half, span] = mul(jnp.concatenate(masks_a, axis=1), stack).astype(BF16)
        inner_ref[half:rows, span] = mul(jnp.concatenate(masks_b, axis=1), stack_b).astype(BF16)
    out_flow[pl.ds(first, group), :] = jnp.concatenate(flows, axis=0)
    pair_sum[0:half, 0:half] += sum_aa
    pair_sum[0:half, half:rows] += sum_ab
    pair_sum[half:rows, half:rows] += sum_bb
    own_ref[0:half, :] += own_a
    own_ref[half:rows, :] += own_b

    @pl.when(turn == pl.num_programs(0) - 1)
    def _():
        net = own_ref[...] - out_flow[...].T
        within_ref[...] = mul_exact(triangle(rows, lambda r, c: r > c), net)
        weighted = scale * pair_sum[...]
        maps_ref[...] = jnp.concatenate(
            [
                mul_exact(weighted, read_ref[...].astype(F32), ((1,), (1,))),
                mul_exact(weighted, write_ref[...].astype(F32), ((0,), (1,))),
            ],
            axis=1,
        )


def carry_kernel(head_width, scale, first_head, parts, first, last, *refs):
    refs = list(refs)
    take = lambda count: [refs.pop(0) for _ in range(count)]
    raw_ref, bias_ref, decay_ref, step_ref, cum_ref, write_ref, read_ref, skip_ref = take(8)
    x_ref, dy_ref, inner_ref, answer_ref = take(4)
    if not first:
        early_sums, early_through, _ = take(3)
    if last:
        own_refs, within_refs, map_refs = take(parts), take(parts), take(parts)
        grad_ref, table_ref, sums, through, weight_e, weight_s, maps = take(7)
    else:
        grad_ref, sums, through, weight_e, weight_s, maps = take(6)
    turn = pl.program_id(0)
    rows, lanes = x_ref.shape
    heads = step_ref.shape[1]
    state = write_ref.shape[0]
    future, past = slice(0, heads), slice(heads, 2 * heads)
    write_sum = slice(2 * heads, 2 * heads + 2 * state)
    read_sum = slice(2 * heads + 2 * state, 2 * heads + 4 * state)

    @pl.when(turn == 0)
    def _():
        cum = cum_ref[...]
        finish = cum[rows - 1 : rows, :]
        top, low = halves(step_ref[...] * jnp.exp(finish - cum) * scale)
        weight_e[...] = jnp.concatenate([top, low], axis=1)
        top, low = halves(jnp.exp(cum) * scale)
        weight_s[...] = jnp.concatenate([top, low], axis=1)
        write = write_ref[...].astype(F32).T.astype(BF16)
        read = read_ref[...].astype(F32).T.astype(BF16)
        maps[...] = jnp.concatenate([write, write, read, read], axis=1)
        if first:
            sums[...] = jnp.zeros_like(sums)
            through[...] = jnp.zeros_like(through)
        else:
            sums[...] = early_sums[...]
            through[...] = early_through[...]

    pick = head_selector(first_head + turn * (lanes // head_width), heads, lanes, head_width)
    pick_twice = jnp.concatenate([pick, pick], axis=0)
    starts, ends = [], []
    for piece in range(answer_ref.shape[0]):
        back = jnp.exp2(-answer_ref[piece, 2 * state : 2 * state + META, :].astype(F32))
        starts.append(decode(answer_ref[piece, 0:state, :]) * back[0:1])
        ends.append(decode(answer_ref[piece, state : 2 * state, :]) * back[1:2])
    start = jnp.concatenate(starts, axis=1)
    end = jnp.concatenate(ends, axis=1)
    start_parts = jnp.concatenate(halves(start), axis=0)
    end_parts = jnp.concatenate(halves(end), axis=0)
    x = x_ref[...].astype(F32)
    dy = dy_ref[...].astype(F32)
    skip = jnp.concatenate(
        [part.astype(F32) for part in thirds(skip_ref[...])] + [jnp.zeros((13, heads), F32)], axis=0
    )
    skip = jnp.sum(mul(skip.astype(BF16), pick), axis=0, keepdims=True)

    spread_e = mul(weight_e[...], pick_twice)
    carried = mul(maps[:, 0 : 2 * state], end_parts) * spread_e
    grad_ref[...] = (inner_ref[...].astype(F32) + skip * dy + carried).astype(BF16)
    top, low = halves(x * carried)
    sums[:, future] += mul_nt(top, pick) + mul_nt(low, pick)
    top, low = halves(x * spread_e)
    sums[:, write_sum] += mul_nt(top, end_parts) + mul_nt(low, end_parts)

    weighted = dy * mul(weight_s[...], pick_twice)
    top, low = halves(weighted * mul(maps[:, 2 * state : 4 * state], start_parts))
    sums[:, past] += mul_nt(top, pick) + mul_nt(low, pick)
    top, low = halves(weighted)
    sums[:, read_sum] += mul_nt(top, start_parts) + mul_nt(low, start_parts)

    both = jnp.broadcast_to(jnp.sum(start * end, axis=0, keepdims=True), (8, lanes))
    top, low = halves(both)
    through[...] += mul_nt(top, pick) + mul_nt(low, pick)

    if not last:
        return

    @pl.when(turn == pl.num_programs(0) - 1)
    def _():
        rate = -jnp.exp(decay_ref[...])
        step = step_ref[...]
        gate = jax.nn.sigmoid(raw_ref[...].astype(F32) + bias_ref[...])
        finish = cum_ref[rows - 1 : rows, :]
        to_come = sums[:, future]
        decay_grad = (
            sum(ref[...] for ref in within_refs)
            + mul_exact(triangle(rows, lambda r, c: r <= c), sums[:, past])
            + mul_exact(triangle(rows, lambda r, c: r > c), to_come)
            + jnp.exp(finish) * scale * through[0:1, :]
        )
        ratio = jnp.where(step > 1e-30, gate / jnp.maximum(step, 1e-30), 1.0)
        inner = sum(ref[...] for ref in own_refs) + to_come
        raw_grad = inner * ratio + rate * decay_grad * gate
        map_sum = sums[:, 2 * heads :] + 0.0
        write_all = map_sum[:, 0:state] + map_sum[:, state : 2 * state]
        read_all = map_sum[:, 2 * state : 3 * state] + map_sum[:, 3 * state :]
        map_grad = jnp.concatenate([write_all, read_all], axis=1)
        map_grad += sum(ref[...] for ref in map_refs)
        table_ref[...] = jnp.concatenate([raw_grad.T, map_grad.T], axis=0).astype(BF16)


def projection_kernel(table_ref, layer_ref, out_ref):
    product = mul(table_ref[...], layer_ref[...])
    width = out_ref.shape[2]
    for piece in range(out_ref.shape[0]):
        out_ref[piece, :, :] = product[:, piece * width : (piece + 1) * width]


def whole(shape):
    return pl.BlockSpec(shape, lambda i: (0,) * len(shape))


def call(kernel, steps, in_specs, out, scratch, flops, bytes_accessed, aliases=None):
    return pl.pallas_call(
        kernel,
        grid=(steps,),
        in_specs=in_specs,
        out_specs=[spec for spec, _, _ in out],
        out_shape=[jax.ShapeDtypeStruct(dims, dtype) for _, dims, dtype in out],
        scratch_shapes=[pltpu.VMEM(dims, dtype) for dims, dtype in scratch],
        compiler_params=pltpu.CompilerParams(vmem_limit_bytes=VMEM_LIMIT),
        cost_estimate=pl.CostEstimate(
            flops=flops, bytes_accessed=bytes_accessed, transcendentals=0
        ),
        input_output_aliases=aliases or {},
    )


def body(
    layer_input,
    head_inputs,
    output_grad,
    step_raw,
    state_write,
    state_read,
    decay_log,
    step_bias,
    skip_gain,
):
    rows, channels = head_inputs.shape
    heads = step_raw.shape[1]
    head_width = channels // heads
    state = state_write.shape[1]
    model = layer_input.shape[1]
    columns = heads + 2 * state
    axes = ("wide", "seq")
    blocks = lax.axis_size("wide") * lax.axis_size("seq")
    scale = float(rows * blocks * state) ** -0.5
    parts = HALVES if heads % (HALVES * blocks) == 0 else 1
    part_heads = heads // parts
    part_lanes = channels // parts
    owner_lanes = part_lanes // blocks
    piece_lanes = max(owner_lanes, 128)
    pieces = part_lanes // piece_lanes
    depth = 2 * state + META
    bias = step_bias[None, :]
    decay = decay_log[None, :]
    skip = skip_gain[None, :]
    write_t, read_t = state_write.T, state_read.T

    lanes = CARRY_HEADS * head_width
    steps = part_lanes // lanes
    here = lanes // piece_lanes

    def tokens(part, width):
        first = part * (part_lanes // width)
        return pl.BlockSpec((rows, width), lambda i: (0, first + i))

    message_spec = pl.BlockSpec((here, depth, piece_lanes), lambda i: (i, 0, 0))
    head_spec = whole((rows, heads))
    line_spec = whole((1, heads))
    map_spec = whole((state, rows))
    head_out = (head_spec, (rows, heads), F32)

    def summaries(part):
        return call(
            functools.partial(summary_kernel, head_width, part * part_heads),
            steps,
            [head_spec, line_spec, line_spec, map_spec, map_spec]
            + [tokens(part, lanes), tokens(part, lanes)],
            [(message_spec, (pieces, depth, piece_lanes), BF16), head_out, head_out],
            [((rows, 2 * heads), BF16), ((rows, 2 * heads), BF16), ((META, heads), BF16)],
            8 * rows * part_lanes * state,
            10 * 2**20 // parts,
        )(step_raw, bias, decay, write_t, read_t, head_inputs, output_grad)

    def exchange(array):
        return lax.all_to_all(array, axes, split_axis=0, concat_axis=0, tiled=True)

    def to_owner(array):
        if owner_lanes < piece_lanes:
            split = array.reshape(pieces, depth, piece_lanes // owner_lanes, owner_lanes)
            array = jnp.moveaxis(split, 2, 1).reshape(blocks, depth, owner_lanes)
        return exchange(array)

    def from_owner(array):
        array = exchange(array)
        if owner_lanes < piece_lanes:
            split = array.reshape(pieces, piece_lanes // owner_lanes, depth, owner_lanes)
            array = jnp.moveaxis(split, 1, 2).reshape(pieces, depth, piece_lanes)
        return array

    def scan(message):
        spec = whole((blocks, depth, owner_lanes))
        (answer,) = call(
            scan_kernel,
            1,
            [spec],
            [(spec, (blocks, depth, owner_lanes), BF16)],
            [((2, blocks, owner_lanes), F32)],
            2**22,
            4 * 2**20 // parts,
        )(message)
        return answer

    def own_block(part, step, cum):
        width = PAIR_HEADS * head_width
        part_spec = pl.BlockSpec((rows, width), lambda i: (0, i))
        return call(
            functools.partial(block_kernel, head_width, scale, part * part_heads),
            part_lanes // width,
            [head_spec, head_spec, map_spec, map_spec, tokens(part, width), tokens(part, width)],
            [
                (part_spec, (rows, part_lanes), BF16),
                head_out,
                head_out,
                (whole((rows, 2 * state)), (rows, 2 * state), F32),
            ],
            [
                ((rows, rows), F32),
                ((rows, heads), F32),
                ((heads, rows), F32),
                ((rows, rows), F32),
                ((heads, rows), F32),
            ],
            16 * rows * rows * part_lanes,
            12 * 2**20 // parts,
        )(step, cum, write_t, read_t, head_inputs, output_grad)

    with jax.named_scope("summaries"):
        summed = [summaries(part) for part in range(parts)]
    step, cum = summed[0][1:]
    with jax.named_scope("own_block"):
        own_parts = [own_block(part, step, cum) for part in range(parts)]
    with jax.named_scope("scan"):
        returned = [from_owner(scan(to_owner(one[0]))) for one in summed]

    sums_out = (whole((rows, 2 * heads + 4 * state)), (rows, 2 * heads + 4 * state), F32)
    through_out = (whole((8, heads)), (8, heads), F32)
    early = ()
    with jax.named_scope("carried"):
        for part in range(parts):
            first, last = part == 0, part == parts - 1
            in_specs = [head_spec, line_spec, line_spec, head_spec, head_spec, map_spec, map_spec]
            in_specs += [line_spec, tokens(part, lanes), tokens(part, lanes)]
            in_specs += [pl.BlockSpec((rows, lanes), lambda i: (0, i)), message_spec]
            operands = [step_raw, bias, decay, step, cum, write_t, read_t, skip]
            operands += [head_inputs, output_grad, own_parts[part][0], returned[part]]
            aliases = {}
            if not first:
                in_specs += [sums_out[0], through_out[0], pl.BlockSpec(memory_space=pl.ANY)]
                operands += [early[1], early[2], early[0]]
                aliases = {len(operands) - 1: 0}
            scratch = [((rows, 2 * heads), BF16)] * 2 + [((rows, 4 * state), BF16)]
            out = [(tokens(part, lanes), (rows, channels), BF16)]
            if last:
                for which in (1, 2, 3):
                    operands += [one[which] for one in own_parts]
                    in_specs += [whole(one[which].shape) for one in own_parts]
                out += [(whole((columns, rows)), (columns, rows), BF16)]
                scratch = [sums_out[1:], through_out[1:]] + scratch
            else:
                out += [sums_out, through_out]
            early = call(
                functools.partial(
                    carry_kernel, head_width, scale, part * part_heads, parts, first, last
                ),
                steps,
                in_specs,
                out,
                scratch,
                32 * rows * part_lanes * state,
                18 * 2**20 // parts,
                aliases,
            )(*operands)
    grad_x, table = early

    with jax.named_scope("projection"):
        own_model = model // blocks
        model_lanes = max(own_model, min(model, 1024))
        (product,) = call(
            projection_kernel,
            model // model_lanes,
            [whole((columns, rows)), pl.BlockSpec((rows, model_lanes), lambda i: (0, i))],
            [
                (
                    pl.BlockSpec((model_lanes // own_model, columns, own_model), lambda i: (i, 0, 0)),
                    (blocks, columns, own_model),
                    F32,
                )
            ],
            [],
            2 * rows * model * columns,
            12 * 2**20,
        )(table, layer_input)
        weight_grad = lax.psum_scatter(
            product, ("seq", "wide"), scatter_dimension=0, tiled=True
        )
    return (grad_x, weight_grad[0].T / math.sqrt(rows * blocks))


def solution(mesh):
    in_specs = (
        P(("wide", "seq"), None),
        P(("wide", "seq"), None),
        P(("wide", "seq"), None),
        P(("wide", "seq"), None),
        P(("wide", "seq"), None),
        P(("wide", "seq"), None),
        P(),
        P(),
        P(),
    )
    out_specs = (P(("wide", "seq"), None), P(("seq", "wide"), None))
    return jax.shard_map(body, mesh=mesh, in_specs=in_specs, out_specs=out_specs, check_vma=False)
```

profile of v0, /device:TPU:0, one launch (start us, length us, event | category | flops | bytes accessed | tf_op | source)
XLA Modules:
  0.0 346.0 jit_solution(9381613179536327807)
XLA Ops:
  7.2 7.2 %summaries.2 = (bf16[32,144,128]{2,1,0:T(8,128)(2,1)}, f32[256,128]{1,0:T(8,128)}, f32[256,128]{1,0:T(8,128)}) custom-call(bf16[256,128]{1,0:T(8,128)(2,1)} %refs_0_.3, f32[1,128]{1,0:T(1,128)} %bitcast.21, f32[1,128]{1,0:T(1,128)} %bitcast.25, bf16[64,256]{1,0:T(8,128)(2,1)} %bitcast.9, bf16[64,256]{1,0:T(8,128)(2,1)} %bitcast.15, ...), custom_call_target="tpu_custom_call" | custom-call | flops 536870912 | bytes 5242880 | tf_op jit(solution)/shard_map/summaries/pallas_call | solution.py:465
  14.4 7.3 %all-to-all-start.2 = ((bf16[32,144,128]{2,1,0:T(8,128)(2,1)}), bf16[32,144,128]{2,1,0:T(8,128)(2,1)S(1)}, u32[]{:S(2)}, u32[]{:S(2)}) async-start(bf16[32,144,128]{2,1,0:T(8,128)(2,1)} %get-tuple-element.24), calls=%async_computation.2 | async-start | bytes 2359296 | tf_op jit(solution)/shard_map/scan/all_to_all | solution.py:477
  21.7 7.2 %summaries.3 = (bf16[32,144,128]{2,1,0:T(8,128)(2,1)}, f32[256,128]{1,0:T(8,128)}, f32[256,128]{1,0:T(8,128)}) custom-call(bf16[256,128]{1,0:T(8,128)(2,1)} %refs_0_.3, f32[1,128]{1,0:T(1,128)} %bitcast.22, f32[1,128]{1,0:T(1,128)} %bitcast.26, bf16[64,256]{1,0:T(8,128)(2,1)} %bitcast.10, bf16[64,256]{1,0:T(8,128)(2,1)} %bitcast.16, ...), custom_call_target="tpu_custom_call" | custom-call | flops 536870912 | bytes 5242880 | tf_op jit(solution)/shard_map/summaries/pallas_call | solution.py:465
  28.9 20.6 %all-to-all-done.2.message_ref = bf16[32,144,128]{2,1,0:T(8,128)(2,1)S(1)} async-done(((bf16[32,144,128]{2,1,0:T(8,128)(2,1)}), bf16[32,144,128]{2,1,0:T(8,128)(2,1)S(1)}, u32[]{:S(2)}, u32[]{:S(2)}) %all-to-all-start.2) | async-done | bytes 1179680 | tf_op jit(solution)/shard_map/scan/all_to_all | solution.py:477
  49.5 0.0 copy-start.2
  49.5 4.5 %all-to-all-start = ((bf16[32,144,128]{2,1,0:T(8,128)(2,1)}), bf16[32,144,128]{2,1,0:T(8,128)(2,1)S(1)}, u32[]{:S(2)}, u32[]{:S(2)}) async-start(bf16[32,144,128]{2,1,0:T(8,128)(2,1)} %get-tuple-element.22), calls=%async_computation | async-start | bytes 2359296 | tf_op jit(solution)/shard_map/scan/all_to_all | solution.py:477
  54.0 0.0 copy-done.2
  54.0 3.9 %scan.3 = bf16[32,144,128]{2,1,0:T(8,128)(2,1)} custom-call(bf16[32,144,128]{2,1,0:T(8,128)(2,1)} %copy-done.2), custom_call_target="tpu_custom_call" | custom-call | flops 4194304 | bytes 2097152 | tf_op jit(solution)/shard_map/scan/pallas_call | solution.py:494
  57.9 23.9 %all-to-all-done.message_ref = bf16[32,144,128]{2,1,0:T(8,128)(2,1)S(1)} async-done(((bf16[32,144,128]{2,1,0:T(8,128)(2,1)}), bf16[32,144,128]{2,1,0:T(8,128)(2,1)S(1)}, u32[]{:S(2)}, u32[]{:S(2)}) %all-to-all-start) | async-done | bytes 1179680 | tf_op jit(solution)/shard_map/scan/all_to_all | solution.py:477
  81.7 0.0 copy-start.3
  81.7 4.5 %all-to-all-start.3 = ((bf16[32,144,128]{2,1,0:T(8,128)(2,1)}), bf16[32,144,128]{2,1,0:T(8,128)(2,1)S(1)}, u32[]{:S(2)}, u32[]{:S(2)}) async-start(bf16[32,144,128]{2,1,0:T(8,128)(2,1)} %scan.3), calls=%async_computation.3 | async-start | bytes 2359296 | tf_op jit(solution)/shard_map/scan/all_to_all | solution.py:477
  86.2 0.0 copy-done.3
  86.3 3.9 %scan.2 = bf16[32,144,128]{2,1,0:T(8,128)(2,1)} custom-call(bf16[32,144,128]{2,1,0:T(8,128)(2,1)} %copy-done.3), custom_call_target="tpu_custom_call" | custom-call | flops 4194304 | bytes 2097152 | tf_op jit(solution)/shard_map/scan/pallas_call | solution.py:494
  90.2 23.9 %all-to-all-done.3.refs_11_ = bf16[32,144,128]{2,1,0:T(8,128)(2,1)S(1)} async-done(((bf16[32,144,128]{2,1,0:T(8,128)(2,1)}), bf16[32,144,128]{2,1,0:T(8,128)(2,1)S(1)}, u32[]{:S(2)}, u32[]{:S(2)}) %all-to-all-start.3) | async-done | bytes 1179680 | tf_op jit(solution)/shard_map/scan/all_to_all | solution.py:477
  114.0 0.0 copy-start.1
  114.0 4.5 %all-to-all-start.1 = ((bf16[32,144,128]{2,1,0:T(8,128)(2,1)}), bf16[32,144,128]{2,1,0:T(8,128)(2,1)S(1)}, u32[]{:S(2)}, u32[]{:S(2)}) async-start(bf16[32,144,128]{2,1,0:T(8,128)(2,1)} %scan.2), calls=%async_computation.1 | async-start | bytes 2359296 | tf_op jit(solution)/shard_map/scan/all_to_all | solution.py:477
  118.5 0.2 reduce-scatter.2.cloned.1.call-start
  118.8 16.3 %own_block.3 = (bf16[256,4096]{1,0:T(8,128)(2,1)}, f32[256,128]{1,0:T(8,128)}, f32[256,128]{1,0:T(8,128)}, f32[256,128]{1,0:T(8,128)}) custom-call(f32[256,128]{1,0:T(8,128)} %get-tuple-element.19.step_ref.refs_3_, f32[256,128]{1,0:T(8,128)} %get-tuple-element.20.cum_ref.refs_4_, bf16[64,256]{1,0:T(8,128)(2,1)} %bitcast.11, bf16[64,256]{1,0:T(8,128)(2,1)} %bitcast.17, ...), custom_call_target="tpu_custom_call" | custom-call | flops 4294967296 | bytes 6291456 | tf_op jit(solution)/shard_map/own_block/pallas_call | solution.py:508
  135.1 0.0 copy-done.1
  135.1 16.6 %own_block.2 = (bf16[256,4096]{1,0:T(8,128)(2,1)}, f32[256,128]{1,0:T(8,128)}, f32[256,128]{1,0:T(8,128)}, f32[256,128]{1,0:T(8,128)}) custom-call(f32[256,128]{1,0:T(8,128)} %get-tuple-element.19.step_ref.refs_3_, f32[256,128]{1,0:T(8,128)} %get-tuple-element.20.cum_ref.refs_4_, bf16[64,256]{1,0:T(8,128)(2,1)} %bitcast.12, bf16[64,256]{1,0:T(8,128)(2,1)} %bitcast.18, ...), custom_call_target="tpu_custom_call" | custom-call | flops 4294967296 | bytes 6291456 | tf_op jit(solution)/shard_map/own_block/pallas_call | solution.py:508
  151.7 12.4 %carried.2 = (bf16[256,8192]{1,0:T(8,128)(2,1)}, f32[256,512]{1,0:T(8,128)}, f32[8,128]{1,0:T(8,128)}) custom-call(bf16[256,128]{1,0:T(8,128)(2,1)} %refs_0_.3, f32[1,128]{1,0:T(1,128)} %bitcast.23, f32[1,128]{1,0:T(1,128)} %bitcast.27, f32[256,128]{1,0:T(8,128)} %get-tuple-element.19.step_ref.refs_3_, f32[256,128]{1,0:T(8,128)} %get-tuple-element.20.cum_ref.refs_4_, ...), custom_call_target="tpu_custom_call" | custom-call | flops 2147483648 | bytes 9437184 | tf_op jit(solution)/shard_map/carried/pallas_call | solution.py:563
  164.2 0.0 all-to-all-done.1.refs_11_
  164.2 0.0 copy-start
  164.2 1.0 copy-done
  165.2 13.7 %carried.3 = (bf16[256,8192]{1,0:T(8,128)(2,1)}, bf16[256,256]{1,0:T(8,128)(2,1)}) custom-call(bf16[256,128]{1,0:T(8,128)(2,1)} %refs_0_.3, f32[1,128]{1,0:T(1,128)} %bitcast.24, f32[1,128]{1,0:T(1,128)} %bitcast.28, f32[256,128]{1,0:T(8,128)} %get-tuple-element.19.step_ref.refs_3_, ...), custom_call_target="tpu_custom_call", output_to_operand_aliasing={{0}: (14, {})} | custom-call | flops 2147483648 | bytes 9437184 | tf_op jit(solution)/shard_map/carried/pallas_call | solution.py:563
  178.9 8.3 %projection.1 = f32[32,256,256]{2,1,0:T(8,128)} custom-call(bf16[256,256]{1,0:T(8,128)(2,1)} %get-tuple-element.35.table_ref, bf16[256,8192]{1,0:T(8,128)(2,1)} %layer_ref.1), custom_call_target="tpu_custom_call" | custom-call | flops 1073741824 | bytes 12582912 | tf_op jit(solution)/shard_map/projection/pallas_call | solution.py:580
  187.2 0.0 reduce-scatter.2.cloned.1.call-update
  187.2 150.1 %reduce-scatter.2.cloned.1.call-done = f32[1,256,256]{2,1,0:T(8,128)} async-done(((f32[32,256,256]{2,1,0:T(8,128)}), f32[1,256,256]{2,1,0:T(8,128)}) %reduce-scatter.2.cloned.1.call-update) | async-done | bytes 262160 | tf_op jit(solution)/shard_map/projection/reduce_scatter | solution.py:595
  337.3 1.0 multiply_bitcast_fusion
  338.3 0.8 copy.12
Async XLA Ops:
  14.4 35.1 %all-to-all-start.2 = ((bf16[32,144,128]{2,1,0:T(8,128)(2,1)}), bf16[32,144,128]{2,1,0:T(8,128)(2,1)S(1)}, u32[]{:S(2)}, u32[]{:S(2)}) async-start(bf16[32,144,128]{2,1,0:T(8,128)(2,1)} %get-tuple-element.24), calls=%async_computation.2 | async-start | bytes 2359296 | tf_op jit(solution)/shard_map/scan/all_to_all | solution.py:477
  49.5 4.5 %copy-start.2 = (bf16[32,144,128]{2,1,0:T(8,128)(2,1)}, bf16[32,144,128]{2,1,0:T(8,128)(2,1)S(1)}, u32[]{:S(2)}) copy-start(bf16[32,144,128]{2,1,0:T(8,128)(2,1)S(1)} %all-to-all-done.2.message_ref) | copy-start | bytes 3538948
  49.5 32.3 %all-to-all-start = ((bf16[32,144,128]{2,1,0:T(8,128)(2,1)}), bf16[32,144,128]{2,1,0:T(8,128)(2,1)S(1)}, u32[]{:S(2)}, u32[]{:S(2)}) async-start(bf16[32,144,128]{2,1,0:T(8,128)(2,1)} %get-tuple-element.22), calls=%async_computation | async-start | bytes 2359296 | tf_op jit(solution)/shard_map/scan/all_to_all | solution.py:477
  81.7 4.5 %copy-start.3 = (bf16[32,144,128]{2,1,0:T(8,128)(2,1)}, bf16[32,144,128]{2,1,0:T(8,128)(2,1)S(1)}, u32[]{:S(2)}) copy-start(bf16[32,144,128]{2,1,0:T(8,128)(2,1)S(1)} %all-to-all-done.message_ref) | copy-start | bytes 3538948
  81.7 32.3 %all-to-all-start.3 = ((bf16[32,144,128]{2,1,0:T(8,128)(2,1)}), bf16[32,144,128]{2,1,0:T(8,128)(2,1)S(1)}, u32[]{:S(2)}, u32[]{:S(2)}) async-start(bf16[32,144,128]{2,1,0:T(8,128)(2,1)} %scan.3), calls=%async_computation.3 | async-start | bytes 2359296 | tf_op jit(solution)/shard_map/scan/all_to_all | solution.py:477
  114.0 21.1 %copy-start.1 = (bf16[32,144,128]{2,1,0:T(8,128)(2,1)}, bf16[32,144,128]{2,1,0:T(8,128)(2,1)S(1)}, u32[]{:S(2)}) copy-start(bf16[32,144,128]{2,1,0:T(8,128)(2,1)S(1)} %all-to-all-done.3.refs_11_) | copy-start | bytes 3538948
  114.0 50.1 %all-to-all-start.1 = ((bf16[32,144,128]{2,1,0:T(8,128)(2,1)}), bf16[32,144,128]{2,1,0:T(8,128)(2,1)S(1)}, u32[]{:S(2)}, u32[]{:S(2)}) async-start(bf16[32,144,128]{2,1,0:T(8,128)(2,1)} %scan.2), calls=%async_computation.1 | async-start | bytes 2359296 | tf_op jit(solution)/shard_map/scan/all_to_all | solution.py:477
  118.5 218.8 %reduce-scatter.2.cloned.1.call-start = ((), (), s32[]{:S(2)}) async-start(), calls=%async_computation.5 | async-start | bytes 8650752 | tf_op jit(solution)/shard_map/projection/reduce_scatter | solution.py:595
  164.2 1.0 copy-start
Sparse Core Ops, SparseCore 0:
  187.3 149.9 reduce-scatter.1
where the time goes:
time: 347 us; the launch traced here: 346 us
  waiting for transfers between devices  218 us (63%)
  Pallas kernels  89.6 us (26%)
  starting transfers between devices  21 us (6%)
  between operations  14.1 us (4%)
    reduce_scatter x1, waiting for transfers between devices, body(): lax.psum_scatter(product, ('seq', 'wide'), scatter_dimension=0, tiled=True)  150 us
    all_to_all x4, waiting for transfers between devices, exchange(): return lax.all_to_all(array, axes, split_axis=0, concat_axis=0, tiled=True)  68.3 us
    pallas_call x2, Pallas kernels, own_block(): call(functools.partial(block_kernel, head_width, scale, part * part_heads...  33 us
    pallas_call x2, Pallas kernels, body(): call(functools.partial(carry_kernel, head_width, scale, part * part_heads...  26.1 us
    all_to_all x4, starting transfers between devices, exchange(): return lax.all_to_all(array, axes, split_axis=0, concat_axis=0, tiled=True)  20.8 us
    pallas_call x2, Pallas kernels, summaries(): call(functools.partial(summary_kernel, head_width, part * part_heads), st...  14.4 us
    pallas_call x1, Pallas kernels, body(): call(projection_kernel, model // model_lanes, [whole((columns, rows)), pl...  8.28 us
    pallas_call x2, Pallas kernels, scan(): call(scan_kernel, 1, [spec], [(spec, (blocks, depth, owner_lanes), BF16)]...  7.81 us
  transfers between devices with their start and end apart: 5, of which 4 were waited for; matrix products, arithmetic and copies ran while one was open for 0% of the time, Pallas kernels for 17%

commit v1 on v0

--- a/solution.py
+++ b/solution.py
@@ -138,7 +138,7 @@
     put(2 * state, mul(facts[...], pick).astype(BF16))
 
 
-def scan_kernel(message_ref, answer_ref, powers):
+def scan_kernel(message_ref, after_ref, answer_ref, powers):
     blocks, double, lanes = message_ref.shape
     state = (double - META) // 2
     top = 2.0**TOP_POWER
@@ -177,6 +177,7 @@
     read_ref,
     x_ref,
     dy_ref,
+    after_ref,
     inner_ref,
     own_ref,
     within_ref,
@@ -291,7 +292,7 @@
     refs = list(refs)
     take = lambda count: [refs.pop(0) for _ in range(count)]
     raw_ref, bias_ref, decay_ref, step_ref, cum_ref, write_ref, read_ref, skip_ref = take(8)
-    x_ref, dy_ref, inner_ref, answer_ref = take(4)
+    x_ref, dy_ref, inner_ref, answer_ref, _ = take(5)
     if not first:
         early_sums, early_through, _ = take(3)
     if last:
@@ -385,14 +386,43 @@
         read_all = map_sum[:, 2 * state : 3 * state] + map_sum[:, 3 * state :]
         map_grad = jnp.concatenate([write_all, read_all], axis=1)
         map_grad += sum(ref[...] for ref in map_refs)
-        table_ref[...] = jnp.concatenate([raw_grad.T, map_grad.T], axis=0).astype(BF16)
-
-
-def projection_kernel(table_ref, layer_ref, out_ref):
-    product = mul(table_ref[...], layer_ref[...])
-    width = out_ref.shape[2]
+        table = jnp.concatenate([raw_grad.T, map_grad.T], axis=0).astype(BF16)
+        for copy in range(table_ref.shape[0]):
+            table_ref[copy, :, :] = table
+
+
+def deal_kernel(layer_ref, after_ref, out_ref):
+    width = out_ref.shape[3]
     for piece in range(out_ref.shape[0]):
-        out_ref[piece, :, :] = product[:, piece * width : (piece + 1) * width]
+        out_ref[piece, 0, :, :] = layer_ref[:, piece * width : (piece + 1) * width]
+
+
+def product_kernel(table_ref, layer_ref, out_ref, total):
+    turn = pl.program_id(0)
+    planes, columns, _ = total.shape
+
+    @pl.when(turn == 0)
+    def _():
+        total[...] = jnp.zeros_like(total)
+
+    for plane in range(planes):
+        total[plane] += mul(table_ref[0], layer_ref[0, plane])
+
+    @pl.when(turn == pl.num_programs(0) - 1)
+    def _():
+        most = jnp.max(jnp.abs(total[...]), axis=(0, 1), keepdims=True)
+        power = power_for(jnp.max(most, axis=2, keepdims=True))
+        out_ref[:, 0:columns, :] = encode(total[...] * jnp.exp2(power))
+        out_ref[:, columns:, :] = jnp.broadcast_to(power, out_ref[:, columns:, :].shape).astype(BF16)
+
+
+def gather_kernel(factor, parts_ref, out_ref):
+    columns = out_ref.shape[1]
+    total = jnp.zeros((columns, out_ref.shape[0]), F32)
+    for plane in range(parts_ref.shape[0]):
+        power = parts_ref[plane, columns:, :].astype(F32)[0:1]
+        total += decode(parts_ref[plane, 0:columns, :]) * jnp.exp2(-power)
+    out_ref[...] = (total * factor).T
 
 
 def whole(shape):
@@ -433,7 +463,9 @@
     model = layer_input.shape[1]
     columns = heads + 2 * state
     axes = ("wide", "seq")
-    blocks = lax.axis_size("wide") * lax.axis_size("seq")
+    wide, planes = lax.axis_size("wide"), lax.axis_size("seq")
+    blocks = wide * planes
+    own_model = model // blocks
     scale = float(rows * blocks * state) ** -0.5
     parts = HALVES if heads % (HALVES * blocks) == 0 else 1
     part_heads = heads // parts
@@ -489,26 +521,27 @@
             array = jnp.moveaxis(split, 1, 2).reshape(pieces, depth, piece_lanes)
         return array
 
-    def scan(message):
+    def scan(message, after):
         spec = whole((blocks, depth, owner_lanes))
         (answer,) = call(
             scan_kernel,
             1,
-            [spec],
+            [spec, pl.BlockSpec(memory_space=pl.ANY)],
             [(spec, (blocks, depth, owner_lanes), BF16)],
             [((2, blocks, owner_lanes), F32)],
             2**22,
             4 * 2**20 // parts,
-        )(message)
+        )(message, after)
         return answer
 
-    def own_block(part, step, cum):
+    def own_block(part, step, cum, after):
         width = PAIR_HEADS * head_width
         part_spec = pl.BlockSpec((rows, width), lambda i: (0, i))
         return call(
             functools.partial(block_kernel, head_width, scale, part * part_heads),
             part_lanes // width,
-            [head_spec, head_spec, map_spec, map_spec, tokens(part, width), tokens(part, width)],
+            [head_spec, head_spec, map_spec, map_spec, tokens(part, width), tokens(part, width)]
+            + [pl.BlockSpec(memory_space=pl.ANY)],
             [
                 (part_spec, (rows, part_lanes), BF16),
                 head_out,
@@ -524,15 +557,32 @@
             ],
             16 * rows * rows * part_lanes,
             12 * 2**20 // parts,
-        )(step, cum, write_t, read_t, head_inputs, output_grad)
+        )(step, cum, write_t, read_t, head_inputs, output_grad, after)
 
     with jax.named_scope("summaries"):
         summed = [summaries(part) for part in range(parts)]
-    step, cum = summed[0][1:]
+    step, cum = summed[-1][1:]
+    with jax.named_scope("layer"):
+        dealt = (wide, planes, rows, own_model)
+        (dealt_out,) = call(
+            deal_kernel,
+            planes,
+            [
+                pl.BlockSpec((rows, wide * own_model), lambda i: (0, i)),
+                pl.BlockSpec(memory_space=pl.ANY),
+            ],
+            [(pl.BlockSpec((wide, 1, rows, own_model), lambda i: (0, i, 0, 0)), dealt, BF16)],
+            [],
+            0,
+            8 * 2**20,
+        )(layer_input, cum)
+        layer_parts = lax.all_to_all(dealt_out, "wide", split_axis=0, concat_axis=0, tiled=True)
     with jax.named_scope("own_block"):
-        own_parts = [own_block(part, step, cum) for part in range(parts)]
+        own_parts = [own_block(part, step, cum, dealt_out) for part in range(parts)]
     with jax.named_scope("scan"):
-        returned = [from_owner(scan(to_owner(one[0]))) for one in summed]
+        returned = [
+            from_owner(scan(to_owner(one[0]), own[1])) for one, own in zip(summed, own_parts)
+        ]
 
     sums_out = (whole((rows, 2 * heads + 4 * state)), (rows, 2 * heads + 4 * state), F32)
     through_out = (whole((8, heads)), (8, heads), F32)
@@ -543,8 +593,10 @@
             in_specs = [head_spec, line_spec, line_spec, head_spec, head_spec, map_spec, map_spec]
             in_specs += [line_spec, tokens(part, lanes), tokens(part, lanes)]
             in_specs += [pl.BlockSpec((rows, lanes), lambda i: (0, i)), message_spec]
+            in_specs += [pl.BlockSpec(memory_space=pl.ANY)]
             operands = [step_raw, bias, decay, step, cum, write_t, read_t, skip]
             operands += [head_inputs, output_grad, own_parts[part][0], returned[part]]
+            operands += [layer_parts]
             aliases = {}
             if not first:
                 in_specs += [sums_out[0], through_out[0], pl.BlockSpec(memory_space=pl.ANY)]
@@ -556,7 +608,7 @@
                 for which in (1, 2, 3):
                     operands += [one[which] for one in own_parts]
                     in_specs += [whole(one[which].shape) for one in own_parts]
-                out += [(whole((columns, rows)), (columns, rows), BF16)]
+                out += [(whole((wide, columns, rows)), (wide, columns, rows), BF16)]
                 scratch = [sums_out[1:], through_out[1:]] + scratch
             else:
                 out += [sums_out, through_out]
@@ -575,27 +627,31 @@
     grad_x, table = early
 
     with jax.named_scope("projection"):
-        own_model = model // blocks
-        model_lanes = max(own_model, min(model, 1024))
+        tables = lax.all_to_all(table, "wide", split_axis=0, concat_axis=0, tiled=True)
+        coded = (planes, columns + META, own_model)
         (product,) = call(
-            projection_kernel,
-            model // model_lanes,
-            [whole((columns, rows)), pl.BlockSpec((rows, model_lanes), lambda i: (0, i))],
+            product_kernel,
+            wide,
             [
-                (
-                    pl.BlockSpec((model_lanes // own_model, columns, own_model), lambda i: (i, 0, 0)),
-                    (blocks, columns, own_model),
-                    F32,
-                )
+                pl.BlockSpec((1, columns, rows), lambda i: (i, 0, 0)),
+                pl.BlockSpec((1, planes, rows, own_model), lambda i: (i, 0, 0, 0)),
             ],
+            [(whole(coded), coded, BF16)],
+            [((planes, columns, own_model), F32)],
+            2 * rows * model * columns,
+            6 * 2**20,
+        )(tables, layer_parts)
+        coded_parts = lax.all_to_all(product, "seq", split_axis=0, concat_axis=0, tiled=True)
+        (weight_grad,) = call(
+            functools.partial(gather_kernel, 1.0 / math.sqrt(rows * blocks)),
+            1,
+            [whole(coded)],
+            [(whole((own_model, columns)), (own_model, columns), F32)],
             [],
-            2 * rows * model * columns,
-            12 * 2**20,
-        )(table, layer_input)
-        weight_grad = lax.psum_scatter(
-            product, ("seq", "wide"), scatter_dimension=0, tiled=True
-        )
-    return (grad_x, weight_grad[0].T / math.sqrt(rows * blocks))
+            2**20,
+            2**20,
+        )(coded_parts)
+    return grad_x, weight_grad
 
 
 def solution(mesh):

time: 347 us -> 258 us (0.74)
  waiting for transfers between devices: 218 us -> 94.8 us
  blocking collectives: 0 us -> 38.8 us
  between operations: 14.1 us -> 0.7 us
  Pallas kernels: 89.6 us -> 96.2 us
  starting transfers between devices: 21 us -> 24.7 us
    reduce_scatter x1 -> x0, waiting for transfers between devices: 150 us -> none  [body(): lax.psum_scatter(product, ('seq', 'wide'), scatter_dimension=0, tiled=True)]
    all_to_all x0 -> x2, blocking collectives: none -> 38.8 us  [the longest x1 19.6 us: body(): lax.all_to_all(table, 'wide', split_axis=0, concat_axis=0, tiled=True)]
    all_to_all x0 -> x1, waiting for transfers between devices: none -> 28.9 us  [body(): lax.all_to_all(dealt_out, 'wide', split_axis=0, concat_axis=0, tiled=True)]
    pallas_call x3 -> x5, Pallas kernels: 16.1 us -> 22.3 us  [the longest x2 7.82 us: scan(): call(scan_kernel, 1, [spec, pl.BlockSpec(memory_space=pl.ANY)], [(spec, (...]
    all_to_all x0 -> x1, starting transfers between devices: none -> 4.56 us  [body(): lax.all_to_all(dealt_out, 'wide', split_axis=0, concat_axis=0, tiled=True)]
  transfers between devices with their start and end apart: 5 -> 5, of which waited for: 4 -> 5; matrix products, arithmetic and copies ran while one was open for 0% -> 0% of each run, Pallas kernels for 17% -> 25%
where the time goes in v1:
time: 258 us; the launch traced here: 257 us
  Pallas kernels  96.2 us (37%)
  waiting for transfers between devices  94.8 us (37%)
  blocking collectives  38.8 us (15%)
  starting transfers between devices  24.7 us (10%)
    all_to_all x4, waiting for transfers between devices, exchange(): return lax.all_to_all(array, axes, split_axis=0, concat_axis=0, tiled=True)  65.9 us
    pallas_call x2, Pallas kernels, own_block(): call(functools.partial(block_kernel, head_width, scale, part * part_heads...  33 us
    all_to_all x1, waiting for transfers between devices, body(): lax.all_to_all(dealt_out, 'wide', split_axis=0, concat_axis=0, tiled=True)  28.9 us
    pallas_call x2, Pallas kernels, body(): call(functools.partial(carry_kernel, head_width, scale, part * part_heads...  26.5 us
    all_to_all x4, starting transfers between devices, exchange(): return lax.all_to_all(array, axes, split_axis=0, concat_axis=0, tiled=True)  20.1 us
    all_to_all x1, blocking collectives, body(): lax.all_to_all(table, 'wide', split_axis=0, concat_axis=0, tiled=True)  19.6 us
    all_to_all x1, blocking collectives, body(): lax.all_to_all(product, 'seq', split_axis=0, concat_axis=0, tiled=True)  19.2 us
    pallas_call x2, Pallas kernels, summaries(): call(functools.partial(summary_kernel, head_width, part * part_heads), st...  14.4 us
  transfers between devices with their start and end apart: 5, of which 5 were waited for; matrix products, arithmetic and copies ran while one was open for 0% of the time, Pallas kernels for 25%

profile of v1, /device:TPU:0, one launch (start us, length us, event | category | flops | bytes accessed | tf_op | source)
XLA Modules:
  0.0 257.3 jit_solution(13091317005086502258)
XLA Ops:
  0.6 7.2 %summaries.2 = (bf16[32,144,128]{2,1,0:T(8,128)(2,1)}, f32[256,128]{1,0:T(8,128)}, f32[256,128]{1,0:T(8,128)}) custom-call(bf16[256,128]{1,0:T(8,128)(2,1)} %refs_0_.3, f32[1,128]{1,0:T(1,128)} %bitcast.17, f32[1,128]{1,0:T(1,128)} %bitcast.21, bf16[64,256]{1,0:T(8,128)(2,1)} %bitcast.5, bf16[64,256]{1,0:T(8,128)(2,1)} %bitcast.11, ...), custom_call_target="tpu_custom_call" | custom-call | flops 536870912 | bytes 5242880 | tf_op jit(solution)/shard_map/summaries/pallas_call | solution.py:497
  7.8 7.3 %all-to-all-start = ((bf16[32,144,128]{2,1,0:T(8,128)(2,1)}), bf16[32,144,128]{2,1,0:T(8,128)(2,1)S(1)}, u32[]{:S(2)}, u32[]{:S(2)}) async-start(bf16[32,144,128]{2,1,0:T(8,128)(2,1)} %get-tuple-element.22), calls=%async_computation | async-start | bytes 2359296 | tf_op jit(solution)/shard_map/scan/all_to_all | solution.py:509
  15.1 7.2 %summaries.3 = (bf16[32,144,128]{2,1,0:T(8,128)(2,1)}, f32[256,128]{1,0:T(8,128)}, f32[256,128]{1,0:T(8,128)}) custom-call(bf16[256,128]{1,0:T(8,128)(2,1)} %refs_0_.3, f32[1,128]{1,0:T(1,128)} %bitcast.18, f32[1,128]{1,0:T(1,128)} %bitcast.22, bf16[64,256]{1,0:T(8,128)(2,1)} %bitcast.6, bf16[64,256]{1,0:T(8,128)(2,1)} %bitcast.12, ...), custom_call_target="tpu_custom_call" | custom-call | flops 536870912 | bytes 5242880 | tf_op jit(solution)/shard_map/summaries/pallas_call | solution.py:497
  22.4 20.6 %all-to-all-done.message_ref = bf16[32,144,128]{2,1,0:T(8,128)(2,1)S(1)} async-done(((bf16[32,144,128]{2,1,0:T(8,128)(2,1)}), bf16[32,144,128]{2,1,0:T(8,128)(2,1)S(1)}, u32[]{:S(2)}, u32[]{:S(2)}) %all-to-all-start) | async-done | bytes 1179680 | tf_op jit(solution)/shard_map/scan/all_to_all | solution.py:509
  42.9 0.0 copy-start.1
  42.9 4.5 %all-to-all-start.3 = ((bf16[32,144,128]{2,1,0:T(8,128)(2,1)}), bf16[32,144,128]{2,1,0:T(8,128)(2,1)S(1)}, u32[]{:S(2)}, u32[]{:S(2)}) async-start(bf16[32,144,128]{2,1,0:T(8,128)(2,1)} %get-tuple-element.25), calls=%async_computation.3 | async-start | bytes 2359296 | tf_op jit(solution)/shard_map/scan/all_to_all | solution.py:509
  47.4 4.8 %layer.1.after_ref = bf16[8,4,256,256]{3,2,1,0:T(8,128)(2,1)} custom-call(bf16[256,8192]{1,0:T(8,128)(2,1)} %layer_ref.1, f32[256,128]{1,0:T(8,128)} %get-tuple-element.20.after_ref.cum_ref.refs_4_), custom_call_target="tpu_custom_call" | custom-call | bytes 8388608 | tf_op jit(solution)/shard_map/layer/pallas_call | solution.py:567
  52.2 0.0 copy-done.1
  52.2 23.0 %all-to-all-done.3.message_ref = bf16[32,144,128]{2,1,0:T(8,128)(2,1)S(1)} async-done(((bf16[32,144,128]{2,1,0:T(8,128)(2,1)}), bf16[32,144,128]{2,1,0:T(8,128)(2,1)S(1)}, u32[]{:S(2)}, u32[]{:S(2)}) %all-to-all-start.3) | async-done | bytes 1179680 | tf_op jit(solution)/shard_map/scan/all_to_all | solution.py:509
  75.2 0.0 copy-start.2
  75.2 1.1 copy-done.2
  76.3 4.6 %all-to-all-start.2 = ((bf16[8,4,256,256]{3,2,1,0:T(8,128)(2,1)}), bf16[8,4,256,256]{3,2,1,0:T(8,128)(2,1)}, u32[]{:S(2)}, u32[]{:S(2)}) async-start(bf16[8,4,256,256]{3,2,1,0:T(8,128)(2,1)} %layer.1.after_ref), calls=%async_computation.2 | async-start | bytes 8388608 | tf_op jit(solution)/shard_map/layer/all_to_all | solution.py:579
  80.8 16.3 %own_block.3 = (bf16[256,4096]{1,0:T(8,128)(2,1)}, f32[256,128]{1,0:T(8,128)}, f32[256,128]{1,0:T(8,128)}, f32[256,128]{1,0:T(8,128)}) custom-call(f32[256,128]{1,0:T(8,128)} %get-tuple-element.19.step_ref.refs_3_, f32[256,128]{1,0:T(8,128)} %get-tuple-element.20.after_ref.cum_ref.refs_4_, bf16[64,256]{1,0:T(8,128)(2,1)} %bitcast.7, ...), custom_call_target="tpu_custom_call" | custom-call | flops 4294967296 | bytes 6291456 | tf_op jit(solution)/shard_map/own_block/pallas_call | solution.py:540
  97.1 3.9 %scan.3 = bf16[32,144,128]{2,1,0:T(8,128)(2,1)} custom-call(bf16[32,144,128]{2,1,0:T(8,128)(2,1)} %copy-done.2, f32[256,128]{1,0:T(8,128)} %get-tuple-element.26.after_ref.refs_16_), custom_call_target="tpu_custom_call" | custom-call | flops 4194304 | bytes 2097152 | tf_op jit(solution)/shard_map/scan/pallas_call | solution.py:526
  101.0 28.9 %all-to-all-done.2.refs_12_.layer_ref = bf16[8,4,256,256]{3,2,1,0:T(8,128)(2,1)} async-done(((bf16[8,4,256,256]{3,2,1,0:T(8,128)(2,1)}), bf16[8,4,256,256]{3,2,1,0:T(8,128)(2,1)}, u32[]{:S(2)}, u32[]{:S(2)}) %all-to-all-start.2) | async-done | bytes 4194336 | tf_op jit(solution)/shard_map/layer/all_to_all | solution.py:579
  129.9 3.6 %all-to-all-start.4 = ((bf16[32,144,128]{2,1,0:T(8,128)(2,1)}), bf16[32,144,128]{2,1,0:T(8,128)(2,1)S(1)}, u32[]{:S(2)}, u32[]{:S(2)}) async-start(bf16[32,144,128]{2,1,0:T(8,128)(2,1)} %scan.3), calls=%async_computation.4 | async-start | bytes 2359296 | tf_op jit(solution)/shard_map/scan/all_to_all | solution.py:509
  133.6 16.7 %own_block.2 = (bf16[256,4096]{1,0:T(8,128)(2,1)}, f32[256,128]{1,0:T(8,128)}, f32[256,128]{1,0:T(8,128)}, f32[256,128]{1,0:T(8,128)}) custom-call(f32[256,128]{1,0:T(8,128)} %get-tuple-element.19.step_ref.refs_3_, f32[256,128]{1,0:T(8,128)} %get-tuple-element.20.after_ref.cum_ref.refs_4_, bf16[64,256]{1,0:T(8,128)(2,1)} %bitcast.8, ...), custom_call_target="tpu_custom_call" | custom-call | flops 4294967296 | bytes 6291456 | tf_op jit(solution)/shard_map/own_block/pallas_call | solution.py:540
  150.3 3.9 %scan.2 = bf16[32,144,128]{2,1,0:T(8,128)(2,1)} custom-call(bf16[32,144,128]{2,1,0:T(8,128)(2,1)} %copy-done.1, f32[256,128]{1,0:T(8,128)} %get-tuple-element.23.after_ref.refs_17_), custom_call_target="tpu_custom_call" | custom-call | flops 4194304 | bytes 2097152 | tf_op jit(solution)/shard_map/scan/pallas_call | solution.py:526
  154.2 7.2 %all-to-all-done.4.refs_11_ = bf16[32,144,128]{2,1,0:T(8,128)(2,1)S(1)} async-done(((bf16[32,144,128]{2,1,0:T(8,128)(2,1)}), bf16[32,144,128]{2,1,0:T(8,128)(2,1)S(1)}, u32[]{:S(2)}, u32[]{:S(2)}) %all-to-all-start.4) | async-done | bytes 1179680 | tf_op jit(solution)/shard_map/scan/all_to_all | solution.py:509
  161.4 0.0 copy-start
  161.4 4.7 %all-to-all-start.1 = ((bf16[32,144,128]{2,1,0:T(8,128)(2,1)}), bf16[32,144,128]{2,1,0:T(8,128)(2,1)S(1)}, u32[]{:S(2)}, u32[]{:S(2)}) async-start(bf16[32,144,128]{2,1,0:T(8,128)(2,1)} %scan.2), calls=%async_computation.1 | async-start | bytes 2359296 | tf_op jit(solution)/shard_map/scan/all_to_all | solution.py:509
  166.0 0.0 copy-done
  166.1 12.4 %carried.2 = (bf16[256,8192]{1,0:T(8,128)(2,1)}, f32[256,512]{1,0:T(8,128)}, f32[8,128]{1,0:T(8,128)}) custom-call(bf16[256,128]{1,0:T(8,128)(2,1)} %refs_0_.3, f32[1,128]{1,0:T(1,128)} %bitcast.19, f32[1,128]{1,0:T(1,128)} %bitcast.23, f32[256,128]{1,0:T(8,128)} %get-tuple-element.19.step_ref.refs_3_, ...), custom_call_target="tpu_custom_call" | custom-call | flops 2147483648 | bytes 9437184 | tf_op jit(solution)/shard_map/carried/pallas_call | solution.py:615
  178.5 15.2 %all-to-all-done.1.refs_11_ = bf16[32,144,128]{2,1,0:T(8,128)(2,1)S(1)} async-done(((bf16[32,144,128]{2,1,0:T(8,128)(2,1)}), bf16[32,144,128]{2,1,0:T(8,128)(2,1)S(1)}, u32[]{:S(2)}, u32[]{:S(2)}) %all-to-all-start.1) | async-done | bytes 1179680 | tf_op jit(solution)/shard_map/scan/all_to_all | solution.py:509
  193.6 0.0 copy-start.3
  193.6 1.0 copy-done.3
  194.7 14.1 %carried.3 = (bf16[256,8192]{1,0:T(8,128)(2,1)}, bf16[8,256,256]{2,1,0:T(8,128)(2,1)}) custom-call(bf16[256,128]{1,0:T(8,128)(2,1)} %refs_0_.3, f32[1,128]{1,0:T(1,128)} %bitcast.20, f32[1,128]{1,0:T(1,128)} %bitcast.24, f32[256,128]{1,0:T(8,128)} %get-tuple-element.19.step_ref.refs_3_, ...), custom_call_target="tpu_custom_call", output_to_operand_aliasing={{0}: (15, {})} | custom-call | flops 2147483648 | bytes 9437184 | tf_op jit(solution)/shard_map/carried/pallas_call | solution.py:615
  208.8 19.6 %all_to_all.35.table_ref = bf16[8,256,256]{2,1,0:T(8,128)(2,1)} all-to-all(bf16[8,256,256]{2,1,0:T(8,128)(2,1)} %get-tuple-element.35), channel_id=1, replica_groups=mesh['seq'=4,'wide'=8] {'wide'}, dimensions={0} | all-to-all | bytes 2097152 | tf_op jit(solution)/shard_map/projection/all_to_all | solution.py:630
  228.4 7.5 %projection.2 = bf16[4,272,256]{2,1,0:T(8,128)(2,1)} custom-call(bf16[8,256,256]{2,1,0:T(8,128)(2,1)} %all_to_all.35.table_ref, bf16[8,4,256,256]{3,2,1,0:T(8,128)(2,1)} %all-to-all-done.2.refs_12_.layer_ref), custom_call_target="tpu_custom_call" | custom-call | flops 1073741824 | bytes 6291456 | tf_op jit(solution)/shard_map/projection/pallas_call | solution.py:632
  235.9 19.2 %all_to_all.36.parts_ref = bf16[4,272,256]{2,1,0:T(8,128)(2,1)} all-to-all(bf16[4,272,256]{2,1,0:T(8,128)(2,1)} %projection.2), channel_id=1, replica_groups=mesh['seq'=4,'wide'=8] {'seq'}, dimensions={0} | all-to-all | bytes 1114112 | tf_op jit(solution)/shard_map/projection/all_to_all | solution.py:644
  255.1 2.2 projection.3
Async XLA Ops:
  7.8 35.1 %all-to-all-start = ((bf16[32,144,128]{2,1,0:T(8,128)(2,1)}), bf16[32,144,128]{2,1,0:T(8,128)(2,1)S(1)}, u32[]{:S(2)}, u32[]{:S(2)}) async-start(bf16[32,144,128]{2,1,0:T(8,128)(2,1)} %get-tuple-element.22), calls=%async_computation | async-start | bytes 2359296 | tf_op jit(solution)/shard_map/scan/all_to_all | solution.py:509
  42.9 9.3 %copy-start.1 = (bf16[32,144,128]{2,1,0:T(8,128)(2,1)}, bf16[32,144,128]{2,1,0:T(8,128)(2,1)S(1)}, u32[]{:S(2)}) copy-start(bf16[32,144,128]{2,1,0:T(8,128)(2,1)S(1)} %all-to-all-done.message_ref) | copy-start | bytes 3538948
  42.9 32.3 %all-to-all-start.3 = ((bf16[32,144,128]{2,1,0:T(8,128)(2,1)}), bf16[32,144,128]{2,1,0:T(8,128)(2,1)S(1)}, u32[]{:S(2)}, u32[]{:S(2)}) async-start(bf16[32,144,128]{2,1,0:T(8,128)(2,1)} %get-tuple-element.25), calls=%async_computation.3 | async-start | bytes 2359296 | tf_op jit(solution)/shard_map/scan/all_to_all | solution.py:509
  75.2 1.1 copy-start.2
  76.3 53.7 %all-to-all-start.2 = ((bf16[8,4,256,256]{3,2,1,0:T(8,128)(2,1)}), bf16[8,4,256,256]{3,2,1,0:T(8,128)(2,1)}, u32[]{:S(2)}, u32[]{:S(2)}) async-start(bf16[8,4,256,256]{3,2,1,0:T(8,128)(2,1)} %layer.1.after_ref), calls=%async_computation.2 | async-start | bytes 8388608 | tf_op jit(solution)/shard_map/layer/all_to_all | solution.py:579
  129.9 31.4 %all-to-all-start.4 = ((bf16[32,144,128]{2,1,0:T(8,128)(2,1)}), bf16[32,144,128]{2,1,0:T(8,128)(2,1)S(1)}, u32[]{:S(2)}, u32[]{:S(2)}) async-start(bf16[32,144,128]{2,1,0:T(8,128)(2,1)} %scan.3), calls=%async_computation.4 | async-start | bytes 2359296 | tf_op jit(solution)/shard_map/scan/all_to_all | solution.py:509
  161.4 4.7 %copy-start = (bf16[32,144,128]{2,1,0:T(8,128)(2,1)}, bf16[32,144,128]{2,1,0:T(8,128)(2,1)S(1)}, u32[]{:S(2)}) copy-start(bf16[32,144,128]{2,1,0:T(8,128)(2,1)S(1)} %all-to-all-done.4.refs_11_) | copy-start | bytes 3538948
  161.4 32.3 %all-to-all-start.1 = ((bf16[32,144,128]{2,1,0:T(8,128)(2,1)}), bf16[32,144,128]{2,1,0:T(8,128)(2,1)S(1)}, u32[]{:S(2)}, u32[]{:S(2)}) async-start(bf16[32,144,128]{2,1,0:T(8,128)(2,1)} %scan.2), calls=%async_computation.1 | async-start | bytes 2359296 | tf_op jit(solution)/shard_map/scan/all_to_all | solution.py:509
  193.6 1.0 copy-start.3
